TPU v7x, 32 devices: a whole 2x2x4 slice. The times are simulated.
32 devices in a mesh: groups: 2 (over x), tx: 16 (over z, y, core).
Axes of the slice: x: 2, y: 2, z: 4, core: 2. Of those that a mesh axis runs over, the one named last changes fastest.
Arguments:
- features: bfloat16 [384, 64, 128], P(('groups', 'tx')), parts along dimension 0, may hold values from -6 to 6
- nbr_table: int32 [384, 27], P(('groups', 'tx')), parts along dimension 0, may hold values from 0 to 20, as said below
- rim_slots: int32 [32, 8], P(('groups', 'tx')), parts along dimension 0, may hold values from 0 to 12, as said below
- w_first: bfloat16 [3456, 128], P('tx'), may hold values from -0.1875 to 0.1875
- w_second: bfloat16 [3456, 128], P('tx'), may hold values from -0.1875 to 0.1875
- cotangent: bfloat16 [384, 64, 128], P(('groups', 'tx')), parts along dimension 0, may hold values from -0.059814453 to 0.059814453
Outputs:
- out_map: bfloat16 [384, 64, 128], P(('groups', 'tx')), parts along dimension 0
- grad_first: float32 [6912, 128], P(('groups', 'tx')), parts along dimension 0
- grad_second: float32 [6912, 128], P(('groups', 'tx')), parts along dimension 0
There are 2 independent parts, one for each index of `groups`. A program takes and returns all parts, laid end to end along the dimension named above; an argument that names none is the same for every part. Nothing has to cross between parts.
Inputs may be any that keep to these rules, and one draw needn't show every extreme that they name: `nbr_table`: A tile's bricks lie in 3 brick rows of 2 by 2 positions; the map strips of tiles t and t+1 touch at t's last and t+1's first brick row. Entry q of an active slot names the brick at brick offset q: a slot of the same tile (0 to 11), 12+i for entry i of the previous tile's last-row list, 12 + 4+i for entry i of the next tile's first-row list, or 20 where that brick is inactive or outside the map; every entry of an empty slot is 20. Some tiles have all 12 slots active. `rim_slots`: each half lists the active bricks of that brick row in order of position, then 12 up to 4 entries; every tile has at least one active brick in its first and in its last brick row, and some tiles have 4 in both.
All inputs are finite; a program needn't handle non-finite values.
Results may differ from a plain program's by a relative error of at most 0.0049.
Values may be sent and summed in bfloat16 or wider, within the bound.
A program may use at most 64 MiB of HBM per device.

v0:
```python
import jax
import jax.numpy as jnp
import numpy as np
from jax import lax
from jax.sharding import PartitionSpec as P

BS = 4


def padded_2(x, sides, width):
    for axis, dim in sides:
        size, length = (lax.axis_size(axis), x.shape[dim])
        up = [(i, (i + 1) % size) for i in range(size - 1)]
        down = [(j, i) for i, j in up]
        last = lax.slice_in_dim(x, length - width, length, axis=dim)
        initial = lax.slice_in_dim(x, 0, width, axis=dim)
        before = lax.ppermute(last, axis, up)
        after = lax.ppermute(initial, axis, down)
        x = jnp.concatenate([before, x, after], axis=dim)
    return x


def brick_tables(side):
    coords = np.arange(side**3)
    first = coords // (side * side)
    second = coords // side % side
    third = coords % side
    brick_code = np.zeros((side**3, 27), np.int32)
    voxel_code = np.zeros((side**3, 27), np.int32)
    for offset in range(27):
        shifts = (offset // 9 - 1, offset // 3 % 3 - 1, offset % 3 - 1)
        code = np.zeros(side**3, np.int32)
        local = np.zeros(side**3, np.int32)
        for along, step in zip((first, second, third), shifts):
            moved = along + step
            brick_step = moved // side
            code = code * 3 + brick_step + 1
            local = local * side + moved - brick_step * side
        brick_code[:, offset] = code
        voxel_code[:, offset] = local
    return (brick_code, voxel_code)


def windows(extended, table, brick_code, voxel_code):
    vox_count = extended.shape[1]
    flat = extended.reshape(-1, extended.shape[2])
    index = table[:, brick_code] * vox_count + jnp.asarray(voxel_code)[None]
    picked = jnp.take(flat, index.reshape(-1).astype(jnp.int32), axis=0)
    return picked.reshape(table.shape[0] * vox_count, -1)


def on_device(features, nbr_table, rim_slots, w_first, w_second, cotangent):
    capacity, vox_count, channels = features.shape
    rim_count = rim_slots.shape[1] // 2
    brick_code, voxel_code = brick_tables(BS)
    zero_brick = jnp.zeros((1, vox_count, channels), jnp.bfloat16)
    own_lists = rim_slots[0]

    def extend(blocks):
        padded = jnp.concatenate([blocks, zero_brick], axis=0)
        packed = jnp.take(padded, own_lists, axis=0)
        beside_all = padded_2(packed, (("tx", 0),), rim_count)
        return jnp.concatenate(
            [blocks, beside_all[:rim_count], beside_all[3 * rim_count :], zero_brick], axis=0
        )

    inputs = windows(extend(features), nbr_table, brick_code, voxel_code)
    piece = lax.all_gather(w_first, "tx", axis=0, tiled=True)
    column_block = lax.slice_in_dim(inputs, 0, piece.shape[0], axis=1)
    first_sum = jnp.dot(column_block, piece, preferred_element_type=jnp.float32)
    hidden = jax.nn.silu(first_sum).astype(jnp.bfloat16)
    second_whole = lax.all_gather(w_second, "tx", axis=0, tiled=True)
    middle = windows(
        extend(hidden.reshape(capacity, vox_count, channels)), nbr_table, brick_code, voxel_code
    )
    out_map = jnp.dot(middle, second_whole, preferred_element_type=jnp.float32).astype(jnp.bfloat16)
    out_map = out_map.reshape(capacity, vox_count, channels)
    cot_rows = cotangent.reshape(-1, channels)
    contract = (((0,), (0,)), ((), ()))
    kernel_count = second_whole.shape[0] // channels
    flipped = (
        second_whole.reshape(kernel_count, channels, channels)[::-1]
        .transpose(0, 2, 1)
        .reshape(-1, channels)
    )
    back = jnp.dot(
        windows(extend(cotangent), nbr_table, brick_code, voxel_code),
        flipped,
        preferred_element_type=jnp.float32,
    )
    sigmoid_mid = jax.nn.sigmoid(first_sum)
    grad_mid = (back * sigmoid_mid * (1.0 + first_sum * (1.0 - sigmoid_mid))).astype(jnp.bfloat16)
    term_second = lax.dot_general(middle, cot_rows, contract, preferred_element_type=jnp.float32)
    term_first = lax.dot_general(inputs, grad_mid, contract, preferred_element_type=jnp.float32)
    grad_first, grad_second = (
        lax.psum_scatter(term_first, "tx", scatter_dimension=0, tiled=True),
        lax.psum_scatter(term_second, "tx", scatter_dimension=0, tiled=True),
    )
    return (out_map, grad_first, grad_second)


def solution(mesh):
    placed = (
        P(("groups", "tx"), None, None),
        P(("groups", "tx"), None),
        P(("groups", "tx"), None),
        P("tx", None),
        P("tx", None),
        P(("groups", "tx"), None, None),
    )
    return jax.shard_map(
        on_device,
        mesh=mesh,
        in_specs=placed,
        out_specs=(
            P(("groups", "tx"), None, None),
            P(("groups", "tx"), None),
            P(("groups", "tx"), None),
        ),
        check_vma=False,
    )
```

profile of v0, /device:TPU:0, one launch (start us, length us, event | category | flops | bytes accessed | tf_op | source)
XLA Modules:
  0.0 361.7 jit_solution(17203760057079737006)
XLA Ops:
  12.4 3.0 collective-permute-start
  15.4 1.3 collective-permute-start.1
  17.3 5.2 %collective-permute-start.4 = (bf16[4,64,128]{2,1,0:T(8,128)(2,1)}, bf16[4,64,128]{2,1,0:T(8,128)(2,1)}, u32[]{:S(2)}, u32[]{:S(2)}) collective-permute-start(bf16[4,64,128]{2,1,0:T(8,128)(2,1)} %get-tuple-element.5), channel_id=1, source_target_pairs={{0,1},{1,2},{2,3},{3,4},{4,5},{5,6},{6,7},{7,8},{8,9},{9,10},{10,1... | collective-permute-start | bytes 196616 | tf_op jit(solution)/shard_map/ppermute | solution.py:17
  22.5 1.3 collective-permute-start.5
  25.3 3.3 gather_fusion
  30.9 27.3 %all_gather.6 = bf16[3456,128]{1,0:T(8,128)(2,1)} all-gather(bf16[216,128]{1,0:T(8,128)(2,1)S(1)} %copy-done.3), channel_id=1, replica_groups=mesh['groups'=2,'tx'=16] {'tx'}, dimensions={0}, use_global_device_ids=true | all-gather | bytes 940032 | tf_op jit(solution)/shard_map/all_gather | solution.py:68
  58.2 19.9 %all_gather.7 = bf16[3456,128]{1,0:T(8,128)(2,1)S(1)} all-gather(bf16[216,128]{1,0:T(8,128)(2,1)S(1)} %copy-done.4), channel_id=1, replica_groups=mesh['groups'=2,'tx'=16] {'tx'}, dimensions={0}, use_global_device_ids=true | all-gather | bytes 940032 | tf_op jit(solution)/shard_map/all_gather | solution.py:72
  78.2 1.3 copy.25
  79.6 1.2 maximum_maximum_fusion.2
  80.8 45.9 %gather_fusion.6 = bf16[20736,128]{1,0:T(8,128)(2,1)} fusion(bf16[1344,128]{1,0:T(8,128)(2,1)S(1)} %bitcast.30, s32[21504]{0:T(1024)} %pad_clamp_fusion), kind=kCustom, calls=%fused_computation.5.clone | custom fusion | bytes 10699776 | tf_op jit(solution)/shard_map/jit(_take)/gather | solution.py:48
  126.8 42.0 %gather_fusion.2 = bf16[20736,128]{1,0:T(8,128)(2,1)} fusion(bf16[1344,128]{1,0:T(8,128)(2,1)S(1)} %bitcast.29, s32[21504]{0:T(1024)S(1)} %copy-done.1), kind=kCustom, calls=%fused_computation.1.clone | custom fusion | bytes 10699776 | tf_op jit(solution)/shard_map/jit(_take)/gather | solution.py:48
  168.8 12.7 %broadcast_select_fusion = (bf16[20736,128]{1,0:T(8,128)(2,1)}, bf16[20736,128]{1,0:T(8,128)(2,1)}) fusion(bf16[20736,128]{1,0:T(8,128)(2,1)} %gather_fusion.6, pred[20736]{0:T(1024)(128)(4,1)S(1)} %copy-done.2, bf16[20736,128]{1,0:T(8,128)(2,1)} %gather_fusion.2), kind=kLoop, calls=%fused_computation.7 | loop fusion | flops 5308416 | bytes 21254400 | tf_op jit(solution)/shard_map/jit(_take)/select_n | solution.py:48
  181.5 10.4 %reshape.69 = bf16[768,3456]{1,0:T(8,128)(2,1)} reshape(bf16[20736,128]{1,0:T(8,128)(2,1)} %get-tuple-element.12) | data formatting | bytes 10616832 | tf_op jit(solution)/shard_map/reshape | solution.py:49
  191.9 10.4 %reshape.75 = bf16[768,3456]{1,0:T(8,128)(2,1)} reshape(bf16[20736,128]{1,0:T(8,128)(2,1)} %get-tuple-element.11) | data formatting | bytes 10616832 | tf_op jit(solution)/shard_map/reshape | solution.py:49
  202.3 4.3 %multiply_convert_fusion = (bf16[768,128]{1,0:T(8,128)(2,1)S(1)}, f32[768,128]{1,0:T(8,128)S(1)}) fusion(bf16[768,3456]{1,0:T(8,128)(2,1)} %reshape.69, bf16[3456,128]{1,0:T(8,128)(2,1)} %all_gather.6), kind=kOutput, calls=%fused_computation.20 | convolution fusion | flops 679968768 | bytes 6782976 | tf_op jit(solution)/shard_map/dot_general | solution.py:70
  207.4 2.3 collective-permute-start.2
  209.6 1.5 collective-permute-start.3
  211.1 10.7 %fusion.2 = f32[3456,128]{1,0:T(8,128)} fusion(bf16[768,3456]{1,0:T(8,128)(2,1)} %reshape.69, bf16[768,3456]{1,0:T(8,128)(2,1)} %reshape.75, bf16[3456,128]{1,0:T(8,128)(2,1)S(1)} %bitcast.33, f32[768,128]{1,0:T(8,128)S(1)} %get-tuple-element.18), kind=kOutput, calls=%fused_computation.15 | convolution fusion | flops 1359839232 | bytes 13664256 | tf_op jit(solution)/shard_map/dot_general | solution.py:94
  222.0 42.0 %gather_fusion.4 = bf16[20736,128]{1,0:T(8,128)(2,1)} fusion(bf16[1344,128]{1,0:T(8,128)(2,1)S(1)} %bitcast.31, s32[21504]{0:T(1024)S(1)} %copy-done.1), kind=kCustom, calls=%fused_computation.4.clone | custom fusion | bytes 10699776 | tf_op jit(solution)/shard_map/jit(_take)/gather | solution.py:48
  264.1 13.9 %broadcast_select_fusion.2 = bf16[20736,128]{1,0:T(8,128)(2,1)} fusion(bf16[20736,128]{1,0:T(8,128)(2,1)} %gather_fusion.4, pred[20736]{0:T(1024)(128)(4,1)S(1)} %copy-done.2), kind=kLoop, calls=%fused_computation.9 | loop fusion | flops 2654208 | bytes 10637568 | tf_op jit(solution)/shard_map/jit(_take)/select_n | solution.py:48
  278.0 10.4 %reshape.72 = bf16[768,3456]{1,0:T(8,128)(2,1)} reshape(bf16[20736,128]{1,0:T(8,128)(2,1)} %broadcast_select_fusion.2) | data formatting | bytes 10616832 | tf_op jit(solution)/shard_map/reshape | solution.py:49
  288.4 5.3 %fusion.11 = f32[3456,128]{1,0:T(8,128)} fusion(bf16[768,3456]{1,0:T(8,128)(2,1)} %reshape.72, bf16[768,128]{1,0:T(8,128)(2,1)S(1)} %bitcast.34), kind=kOutput, calls=%fused_computation.41 | convolution fusion | flops 679477248 | bytes 7274496 | tf_op jit(solution)/shard_map/dot_general | solution.py:93
  293.8 4.7 %convolution_convert_fusion = bf16[768,128]{1,0:T(8,128)(2,1)} fusion(bf16[768,3456]{1,0:T(8,128)(2,1)} %reshape.72, bf16[3456,128]{1,0:T(8,128)(2,1)S(1)} %all_gather.7), kind=kOutput, calls=%fused_computation.13 | convolution fusion | flops 679575552 | bytes 6389760 | tf_op jit(solution)/shard_map/dot_general | solution.py:76
  298.5 56.3 %reduce-scatter.9.cloned.1.call-done = f32[216,128]{1,0:T(8,128)} async-done(((f32[3456,128]{1,0:T(8,128)}), f32[216,128]{1,0:T(8,128)}) %reduce-scatter.9.cloned.1.call-update) | async-done | bytes 110608
  (50 shorter events, 10.7 us)
Async XLA Ops:
  7.2 22.1 %copy-start.5 = (s32[64,27]{1,0:T(8,128)S(1)}, s32[64,27]{1,0:T(8,128)}, u32[]{:S(2)}) copy-start(s32[64,27]{1,0:T(8,128)} %constant.22.clone) | copy-start | bytes 20740
  7.2 23.7 %copy-start.3 = (bf16[216,128]{1,0:T(8,128)(2,1)S(1)}, bf16[216,128]{1,0:T(8,128)(2,1)}, u32[]{:S(2)}) copy-start(bf16[216,128]{1,0:T(8,128)(2,1)} %param.18) | copy-start | bytes 165892
  7.2 51.0 %copy-start.4 = (bf16[216,128]{1,0:T(8,128)(2,1)S(1)}, bf16[216,128]{1,0:T(8,128)(2,1)}, u32[]{:S(2)}) copy-start(bf16[216,128]{1,0:T(8,128)(2,1)} %param.19) | copy-start | bytes 165892
  7.2 291.3 %reduce-scatter.7.cloned.1.call-start = ((), (), s32[]{:S(2)}) async-start(), calls=%async_computation.2 | async-start | bytes 1880064
  12.4 67.2 %collective-permute-start = (bf16[4,64,128]{2,1,0:T(8,128)(2,1)}, bf16[4,64,128]{2,1,0:T(8,128)(2,1)}, u32[]{:S(2)}, u32[]{:S(2)}) collective-permute-start(bf16[4,64,128]{2,1,0:T(8,128)(2,1)} %get-tuple-element.9), channel_id=1, source_target_pairs={{0,1},{1,2},{2,3},{3,4},{4,5},{5,6},{6,7},{7,8},{8,9},{9,10},{10,1... | collective-permute-start | bytes 196616 | tf_op jit(solution)/shard_map/ppermute | solution.py:17
  15.4 64.3 %collective-permute-start.1 = (bf16[4,64,128]{2,1,0:T(8,128)(2,1)}, bf16[4,64,128]{2,1,0:T(8,128)(2,1)}, u32[]{:S(2)}, u32[]{:S(2)}) collective-permute-start(bf16[4,64,128]{2,1,0:T(8,128)(2,1)} %get-tuple-element.10), channel_id=1, source_target_pairs={{1,0},{2,1},{3,2},{4,3},{5,4},{6,5},{7,6},{8,7},{9,8},{10,9},{11,1... | collective-permute-start | bytes 196616 | tf_op jit(solution)/shard_map/ppermute | solution.py:18
  17.3 62.3 %collective-permute-start.4 = (bf16[4,64,128]{2,1,0:T(8,128)(2,1)}, bf16[4,64,128]{2,1,0:T(8,128)(2,1)}, u32[]{:S(2)}, u32[]{:S(2)}) collective-permute-start(bf16[4,64,128]{2,1,0:T(8,128)(2,1)} %get-tuple-element.5), channel_id=1, source_target_pairs={{0,1},{1,2},{2,3},{3,4},{4,5},{5,6},{6,7},{7,8},{8,9},{9,10},{10,1... | collective-permute-start | bytes 196616 | tf_op jit(solution)/shard_map/ppermute | solution.py:17
  22.5 57.1 %collective-permute-start.5 = (bf16[4,64,128]{2,1,0:T(8,128)(2,1)}, bf16[4,64,128]{2,1,0:T(8,128)(2,1)}, u32[]{:S(2)}, u32[]{:S(2)}) collective-permute-start(bf16[4,64,128]{2,1,0:T(8,128)(2,1)} %get-tuple-element.6), channel_id=1, source_target_pairs={{1,0},{2,1},{3,2},{4,3},{5,4},{6,5},{7,6},{8,7},{9,8},{10,9},{11,1... | collective-permute-start | bytes 196616 | tf_op jit(solution)/shard_map/ppermute | solution.py:18
  28.5 51.1 %copy-start = (bf16[12,64,128]{2,1,0:T(8,128)(2,1)S(1)}, bf16[12,64,128]{2,1,0:T(8,128)(2,1)}, u32[]{:S(2)}) copy-start(bf16[12,64,128]{2,1,0:T(8,128)(2,1)} %param.20) | copy-start | bytes 589828
  80.8 46.0 %copy-start.1 = (s32[21504]{0:T(1024)S(1)}, s32[21504]{0:T(1024)}, u32[]{:S(2)}) copy-start(s32[21504]{0:T(1024)} %pad_clamp_fusion) | copy-start | bytes 258052
  126.8 42.1 %copy-start.2 = (pred[20736]{0:T(1024)(128)(4,1)S(1)}, pred[20736]{0:T(1024)(128)(4,1)}, u32[]{:S(2)}) copy-start(pred[20736]{0:T(1024)(128)(4,1)} %compare_and_fusion) | copy-start | bytes 62212
  207.4 14.6 %collective-permute-start.2 = (bf16[4,64,128]{2,1,0:T(8,128)(2,1)S(1)}, bf16[4,64,128]{2,1,0:T(8,128)(2,1)S(1)}, u32[]{:S(2)}, u32[]{:S(2)}) collective-permute-start(bf16[4,64,128]{2,1,0:T(8,128)(2,1)S(1)} %get-tuple-element.7), channel_id=1, source_target_pairs={{0,1},{1,2},{2,3},{3,4},{4,5},{5,6},{6,7},{7,8},{8,9},{9,10},{10,1... | collective-permute-start | bytes 196616 | tf_op jit(solution)/shard_map/ppermute | solution.py:17
  209.6 12.3 %collective-permute-start.3 = (bf16[4,64,128]{2,1,0:T(8,128)(2,1)S(1)}, bf16[4,64,128]{2,1,0:T(8,128)(2,1)S(1)}, u32[]{:S(2)}, u32[]{:S(2)}) collective-permute-start(bf16[4,64,128]{2,1,0:T(8,128)(2,1)S(1)} %get-tuple-element.8), channel_id=1, source_target_pairs={{1,0},{2,1},{3,2},{4,3},{5,4},{6,5},{7,6},{8,7},{9,8},{10,9},{11,1... | collective-permute-start | bytes 196616 | tf_op jit(solution)/shard_map/ppermute | solution.py:18
  221.9 132.9 %reduce-scatter.9.cloned.1.call-start = ((), (), s32[]{:S(2)}) async-start(), calls=%async_computation.3 | async-start | bytes 1880064
Sparse Core Ops, SparseCore 0:
  222.0 60.9 reduce-scatter.6
  293.9 60.8 reduce-scatter.8
where the time goes:
time: 365 us; the launch traced here: 362 us
  local copies, waits for them, and re-layouts  173 us (47%)
  waiting for transfers between devices  56.4 us (15%)
  blocking collectives  47.2 us (13%)
  other arithmetic  31.4 us (9%)
  matrix products  25.1 us (7%)
  starting transfers between devices  14.5 us (4%)
  between operations  14.3 us (4%)
    gather x3, local copies, waits for them, and re-layouts, windows(): picked = jnp.take(flat, index.reshape(-1).astype(jnp.int32), axis=0)  130 us
    unnamed x4, waiting for transfers between devices  56.4 us
    reshape x3, local copies, waits for them, and re-layouts, windows(): return picked.reshape(table.shape[0] * vox_count, -1)  31.3 us
    all_gather x1, blocking collectives, on_device(): piece = lax.all_gather(w_first, 'tx', axis=0, tiled=True)  27.3 us
    select_n x3, other arithmetic, windows(): picked = jnp.take(flat, index.reshape(-1).astype(jnp.int32), axis=0)  26.5 us
    all_gather x1, blocking collectives, on_device(): second_whole = lax.all_gather(w_second, 'tx', axis=0, tiled=True)  19.9 us
    dot_general x1, matrix products, on_device(): lax.dot_general(inputs, grad_mid, contract, preferred_element_type=jnp.fl...  10.7 us
    ppermute x3, starting transfers between devices, padded_2(): before = lax.ppermute(last, axis, up)  10.4 us
  transfers between devices with their start and end apart: 8, of which 1 were waited for; matrix products, arithmetic and copies ran while one was open for 27% of the time, Pallas kernels for 0%

commit v1 on v0

--- a/solution.py
+++ b/solution.py
@@ -5,6 +5,39 @@
 from jax.sharding import PartitionSpec as P
 
 BS = 4
+
+
+def form_sections_here(here_x):
+    chip_axis = "tx"
+    outcome_arr, part_now, spare = (
+        lax.axis_size(chip_axis),
+        lax.axis_index(chip_axis),
+        here_x.shape[0],
+    )
+    runs = tuple((dev * outcome_arr if jj == 0 else dev for jj, dev in enumerate(here_x.shape)))
+    state_next = lax.dynamic_update_slice_in_dim(
+        jnp.zeros(runs, here_x.dtype), here_x, part_now * spare, axis=0
+    )
+    arr_next = everything = here_x
+    for to_i in tuple(range(1, outcome_arr // 2 + 1)):
+        arr_next = lax.ppermute(
+            arr_next,
+            axis_name=chip_axis,
+            perm=tuple(((jj, (jj + 1) % outcome_arr) for jj in range(outcome_arr))),
+        )
+        state_next = lax.dynamic_update_slice_in_dim(
+            state_next, arr_next, (part_now - to_i) % outcome_arr * spare, axis=0
+        )
+        if 2 * to_i < outcome_arr:
+            everything = lax.ppermute(
+                everything,
+                axis_name=chip_axis,
+                perm=tuple(((jj, (jj - 1) % outcome_arr) for jj in range(outcome_arr))),
+            )
+            state_next = lax.dynamic_update_slice_in_dim(
+                state_next, everything, (part_now + to_i) % outcome_arr * spare, axis=0
+            )
+    return state_next
 
 
 def padded_2(x, sides, width):
@@ -69,7 +102,7 @@
     column_block = lax.slice_in_dim(inputs, 0, piece.shape[0], axis=1)
     first_sum = jnp.dot(column_block, piece, preferred_element_type=jnp.float32)
     hidden = jax.nn.silu(first_sum).astype(jnp.bfloat16)
-    second_whole = lax.all_gather(w_second, "tx", axis=0, tiled=True)
+    second_whole = form_sections_here(w_second)
     middle = windows(
         extend(hidden.reshape(capacity, vox_count, channels)), nbr_table, brick_code, voxel_code
     )

time: 365 us -> 394 us (1.079)
  waiting for transfers between devices: 56.4 us -> 86.9 us
  starting transfers between devices: 14.5 us -> 42 us
  blocking collectives: 47.2 us -> 24 us
    ppermute x0 -> x15, starting transfers between devices: none -> 32.3 us  [the longest x7 29.3 us: form_sections_here(): lax.ppermute(everything, axis_name=chip_axis, perm=tuple(((jj, (jj - 1) %...]
    all_gather x1 -> x0, blocking collectives: 19.9 us -> none  [on_device(): second_whole = lax.all_gather(w_second, 'tx', axis=0, tiled=True)]
    unnamed x4, waiting for transfers between devices: 56.4 us -> 72.6 us
    ppermute x0 -> x15, waiting for transfers between devices: none -> 14.3 us  [the longest x8 14.2 us: form_sections_here(): lax.ppermute(arr_next, axis_name=chip_axis, perm=tuple(((jj, (jj + 1) % o...]
    ppermute x3, starting transfers between devices: 10.4 us -> 5.75 us  [padded_2(): before = lax.ppermute(last, axis, up)]
  transfers between devices with their start and end apart: 8 -> 23, of which waited for: 1 -> 7; matrix products, arithmetic and copies ran while one was open for 27% -> 57% of each run, Pallas kernels for 0% -> 0%
where the time goes in v1:
time: 394 us; the launch traced here: 392 us
  local copies, waits for them, and re-layouts  170 us (43%)
  waiting for transfers between devices  86.9 us (22%)
  starting transfers between devices  42 us (11%)
  other arithmetic  29.1 us (7%)
  matrix products  25.8 us (7%)
  blocking collectives  24 us (6%)
  between operations  14.7 us (4%)
    gather x3, local copies, waits for them, and re-layouts, windows(): picked = jnp.take(flat, index.reshape(-1).astype(jnp.int32), axis=0)  127 us
    unnamed x4, waiting for transfers between devices  72.6 us
    reshape x3, local copies, waits for them, and re-layouts, windows(): return picked.reshape(table.shape[0] * vox_count, -1)  31.3 us
    ppermute x7, starting transfers between devices, form_sections_here(): lax.ppermute(everything, axis_name=chip_axis, perm=tuple(((jj, (jj - 1) %...  29.3 us
    select_n x3, other arithmetic, windows(): picked = jnp.take(flat, index.reshape(-1).astype(jnp.int32), axis=0)  26.5 us
    all_gather x1, blocking collectives, on_device(): piece = lax.all_gather(w_first, 'tx', axis=0, tiled=True)  24 us
    ppermute x8, waiting for transfers between devices, form_sections_here(): lax.ppermute(arr_next, axis_name=chip_axis, perm=tuple(((jj, (jj + 1) % o...  14.2 us
    dot_general x1, matrix products, on_device(): lax.dot_general(inputs, grad_mid, contract, preferred_element_type=jnp.fl...  10.8 us
  transfers between devices with their start and end apart: 23, of which 7 were waited for; matrix products, arithmetic and copies ran while one was open for 57% of the time, Pallas kernels for 0%

profile of v1, /device:TPU:0, one launch (start us, length us, event | category | flops | bytes accessed | tf_op | source)
XLA Modules:
  0.0 392.1 jit_solution(13989168752836242490)
XLA Ops:
  7.7 5.1 %collective-permute-start.5 = (bf16[216,128]{1,0:T(8,128)(2,1)}, bf16[216,128]{1,0:T(8,128)(2,1)S(1)}, u32[]{:S(2)}, u32[]{:S(2)}) collective-permute-start(bf16[216,128]{1,0:T(8,128)(2,1)} %param.19), channel_id=1, source_target_pairs={{0,15},{1,0},{2,1},{3,2},{4,3},{5,4},{6,5},{7,6},{8,7},{9,8},{10,9... | collective-permute-start | bytes 165896 | tf_op jit(solution)/shard_map/ppermute | solution.py:32
  24.6 3.3 gather_fusion
  29.0 24.0 %all_gather.3 = bf16[3456,128]{1,0:T(8,128)(2,1)S(1)} all-gather(bf16[216,128]{1,0:T(8,128)(2,1)S(1)} %copy-done.4), channel_id=1, replica_groups=mesh['groups'=2,'tx'=16] {'tx'}, dimensions={0}, use_global_device_ids=true | all-gather | bytes 940032 | tf_op jit(solution)/shard_map/all_gather | solution.py:101
  56.8 3.3 collective-permute-start.7
  60.3 42.3 %gather_fusion.6 = bf16[20736,128]{1,0:T(8,128)(2,1)} fusion(bf16[1344,128]{1,0:T(8,128)(2,1)S(1)} %bitcast.30, s32[21504]{0:T(1024)S(1)} %pad_clamp_fusion), kind=kCustom, calls=%fused_computation.5.clone | custom fusion | bytes 10699776 | tf_op jit(solution)/shard_map/jit(_take)/gather | solution.py:81
  102.6 42.3 %gather_fusion.2 = bf16[20736,128]{1,0:T(8,128)(2,1)} fusion(bf16[1344,128]{1,0:T(8,128)(2,1)S(1)} %bitcast.29, s32[21504]{0:T(1024)S(1)} %pad_clamp_fusion), kind=kCustom, calls=%fused_computation.1.clone | custom fusion | bytes 10699776 | tf_op jit(solution)/shard_map/jit(_take)/gather | solution.py:81
  144.9 12.7 %broadcast_select_fusion = (bf16[20736,128]{1,0:T(8,128)(2,1)}, bf16[20736,128]{1,0:T(8,128)(2,1)}) fusion(bf16[20736,128]{1,0:T(8,128)(2,1)} %gather_fusion.6, pred[20736]{0:T(1024)(128)(4,1)S(1)} %compare_and_fusion, bf16[20736,128]{1,0:T(8,128)(2,1)} %gather_fusion.2), kind=kLoop, calls=%fused_computation.7 | loop fusion | flops 5308416 | bytes 21254400 | tf_op jit(solution)/shard_map/jit(_take)/select_n | solution.py:81
  157.6 10.4 %reshape.69 = bf16[768,3456]{1,0:T(8,128)(2,1)} reshape(bf16[20736,128]{1,0:T(8,128)(2,1)} %get-tuple-element.12) | data formatting | bytes 10616832 | tf_op jit(solution)/shard_map/reshape | solution.py:82
  168.1 4.8 %multiply_convert_fusion = (bf16[768,128]{1,0:T(8,128)(2,1)S(1)}, f32[768,128]{1,0:T(8,128)}) fusion(bf16[768,3456]{1,0:T(8,128)(2,1)} %reshape.69, bf16[3456,128]{1,0:T(8,128)(2,1)S(1)} %all_gather.3), kind=kOutput, calls=%fused_computation.20 | convolution fusion | flops 679968768 | bytes 6782976 | tf_op jit(solution)/shard_map/dot_general | solution.py:103
  176.2 10.4 %reshape.75 = bf16[768,3456]{1,0:T(8,128)(2,1)} reshape(bf16[20736,128]{1,0:T(8,128)(2,1)} %get-tuple-element.11) | data formatting | bytes 10616832 | tf_op jit(solution)/shard_map/reshape | solution.py:82
  187.9 3.2 collective-permute-start.9
  191.2 42.3 %gather_fusion.4 = bf16[20736,128]{1,0:T(8,128)(2,1)} fusion(bf16[1344,128]{1,0:T(8,128)(2,1)S(1)} %bitcast.31, s32[21504]{0:T(1024)S(1)} %pad_clamp_fusion), kind=kCustom, calls=%fused_computation.4.clone | custom fusion | bytes 10699776 | tf_op jit(solution)/shard_map/jit(_take)/gather | solution.py:81
  233.5 13.8 %broadcast_select_fusion.2 = bf16[20736,128]{1,0:T(8,128)(2,1)} fusion(bf16[20736,128]{1,0:T(8,128)(2,1)} %gather_fusion.4, pred[20736]{0:T(1024)(128)(4,1)S(1)} %compare_and_fusion), kind=kLoop, calls=%fused_computation.9 | loop fusion | flops 2654208 | bytes 10637568 | tf_op jit(solution)/shard_map/jit(_take)/select_n | solution.py:81
  247.3 10.4 %reshape.72 = bf16[768,3456]{1,0:T(8,128)(2,1)} reshape(bf16[20736,128]{1,0:T(8,128)(2,1)} %broadcast_select_fusion.2) | data formatting | bytes 10616832 | tf_op jit(solution)/shard_map/reshape | solution.py:82
  257.8 5.4 %fusion.11 = f32[3456,128]{1,0:T(8,128)} fusion(bf16[768,3456]{1,0:T(8,128)(2,1)} %reshape.72, bf16[768,128]{1,0:T(8,128)(2,1)S(1)} %bitcast.34), kind=kOutput, calls=%fused_computation.57 | convolution fusion | flops 679477248 | bytes 7274496 | tf_op jit(solution)/shard_map/dot_general | solution.py:126
  263.4 4.4 %collective-permute-start.11 = (bf16[216,128]{1,0:T(8,128)(2,1)S(1)}, bf16[216,128]{1,0:T(8,128)(2,1)S(1)}, u32[]{:S(2)}, u32[]{:S(2)}) collective-permute-start(bf16[216,128]{1,0:T(8,128)(2,1)S(1)} %collective-permute-done.9), channel_id=1, source_target_pairs={{0,15},{1,0},{2,1},{3,2},{4,3},{5,4},{6,5},{7,6},{8,7},{9,8},{10,9... | collective-permute-start | bytes 165896 | tf_op jit(solution)/shard_map/ppermute | solution.py:32
  269.6 4.4 %collective-permute-start.13 = (bf16[216,128]{1,0:T(8,128)(2,1)S(1)}, bf16[216,128]{1,0:T(8,128)(2,1)S(1)}, u32[]{:S(2)}, u32[]{:S(2)}) collective-permute-start(bf16[216,128]{1,0:T(8,128)(2,1)S(1)} %collective-permute-done.11), channel_id=1, source_target_pairs={{0,15},{1,0},{2,1},{3,2},{4,3},{5,4},{6,5},{7,6},{8,7},{9,8},{10,9... | collective-permute-start | bytes 165896 | tf_op jit(solution)/shard_map/ppermute | solution.py:32
  275.9 4.4 %collective-permute-start.15 = (bf16[216,128]{1,0:T(8,128)(2,1)S(1)}, bf16[216,128]{1,0:T(8,128)(2,1)S(1)}, u32[]{:S(2)}, u32[]{:S(2)}) collective-permute-start(bf16[216,128]{1,0:T(8,128)(2,1)S(1)} %collective-permute-done.13), channel_id=1, source_target_pairs={{0,15},{1,0},{2,1},{3,2},{4,3},{5,4},{6,5},{7,6},{8,7},{9,8},{10,9... | collective-permute-start | bytes 165896 | tf_op jit(solution)/shard_map/ppermute | solution.py:32
  282.2 4.4 %collective-permute-start.17 = (bf16[216,128]{1,0:T(8,128)(2,1)S(1)}, bf16[216,128]{1,0:T(8,128)(2,1)S(1)}, u32[]{:S(2)}, u32[]{:S(2)}) collective-permute-start(bf16[216,128]{1,0:T(8,128)(2,1)S(1)} %collective-permute-done.15), channel_id=1, source_target_pairs={{0,15},{1,0},{2,1},{3,2},{4,3},{5,4},{6,5},{7,6},{8,7},{9,8},{10,9... | collective-permute-start | bytes 165896 | tf_op jit(solution)/shard_map/ppermute | solution.py:32
  288.5 7.0 %collective-permute-done.18 = bf16[216,128]{1,0:T(8,128)(2,1)S(1)} collective-permute-done((bf16[216,128]{1,0:T(8,128)(2,1)S(1)}, bf16[216,128]{1,0:T(8,128)(2,1)S(1)}, u32[]{:S(2)}, u32[]{:S(2)}) %collective-permute-start.18) | collective-permute-done | bytes 55328 | tf_op jit(solution)/shard_map/ppermute | solution.py:23
  297.0 10.8 %fusion.2 = f32[3456,128]{1,0:T(8,128)} fusion(bf16[768,3456]{1,0:T(8,128)(2,1)} %reshape.69, bf16[768,3456]{1,0:T(8,128)(2,1)} %reshape.75, bf16[3456,128]{1,0:T(8,128)(2,1)S(1)} %bitcast.33, f32[768,128]{1,0:T(8,128)S(1)} %copy-done.2), kind=kOutput, calls=%fused_computation.15 | convolution fusion | flops 1359839232 | bytes 13664256 | tf_op jit(solution)/shard_map/dot_general | solution.py:127
  307.9 4.8 %convolution_convert_fusion = bf16[768,128]{1,0:T(8,128)(2,1)} fusion(bf16[768,3456]{1,0:T(8,128)(2,1)} %reshape.72, bf16[3456,128]{1,0:T(8,128)(2,1)S(1)} %constant_dynamic-update-slice_fusion), kind=kOutput, calls=%fused_computation.13 | convolution fusion | flops 679575552 | bytes 6389760 | tf_op jit(solution)/shard_map/dot_general | solution.py:109
  312.7 9.1 %reduce-scatter.9.cloned.1.call-done = f32[216,128]{1,0:T(8,128)} async-done(((f32[3456,128]{1,0:T(8,128)}), f32[216,128]{1,0:T(8,128)}) %reduce-scatter.9.cloned.1.call-update) | async-done | bytes 110608
  321.8 63.5 %reduce-scatter.7.cloned.1.call-done = f32[216,128]{1,0:T(8,128)} async-done(((f32[3456,128]{1,0:T(8,128)}), f32[216,128]{1,0:T(8,128)}) %reduce-scatter.7.cloned.1.call-update) | async-done | bytes 110608
  (96 shorter events, 30.6 us)
Async XLA Ops:
  7.2 314.6 %reduce-scatter.9.cloned.1.call-start = ((), (), s32[]{:S(2)}) async-start(), calls=%async_computation.3 | async-start | bytes 1880064
  7.2 46.3 %collective-permute-start.4 = (bf16[216,128]{1,0:T(8,128)(2,1)}, bf16[216,128]{1,0:T(8,128)(2,1)}, u32[]{:S(2)}, u32[]{:S(2)}) collective-permute-start(bf16[216,128]{1,0:T(8,128)(2,1)} %param.19), channel_id=1, source_target_pairs={{0,1},{1,2},{2,3},{3,4},{4,5},{5,6},{6,7},{7,8},{8,9},{9,10},{10,1... | collective-permute-start | bytes 165896 | tf_op jit(solution)/shard_map/ppermute | solution.py:23
  7.7 47.9 %collective-permute-start.5 = (bf16[216,128]{1,0:T(8,128)(2,1)}, bf16[216,128]{1,0:T(8,128)(2,1)S(1)}, u32[]{:S(2)}, u32[]{:S(2)}) collective-permute-start(bf16[216,128]{1,0:T(8,128)(2,1)} %param.19), channel_id=1, source_target_pairs={{0,15},{1,0},{2,1},{3,2},{4,3},{5,4},{6,5},{7,6},{8,7},{9,8},{10,9... | collective-permute-start | bytes 165896 | tf_op jit(solution)/shard_map/ppermute | solution.py:32
  17.2 43.0 %copy-start = (bf16[12,64,128]{2,1,0:T(8,128)(2,1)S(1)}, bf16[12,64,128]{2,1,0:T(8,128)(2,1)}, u32[]{:S(2)}) copy-start(bf16[12,64,128]{2,1,0:T(8,128)(2,1)} %param.20) | copy-start | bytes 589828
  17.3 39.5 %collective-permute-start = (bf16[4,64,128]{2,1,0:T(8,128)(2,1)S(1)}, bf16[4,64,128]{2,1,0:T(8,128)(2,1)S(1)}, u32[]{:S(2)}, u32[]{:S(2)}) collective-permute-start(bf16[4,64,128]{2,1,0:T(8,128)(2,1)S(1)} %get-tuple-element.9), channel_id=1, source_target_pairs={{0,1},{1,2},{2,3},{3,4},{4,5},{5,6},{6,7},{7,8},{8,9},{9,10},{10,1... | collective-permute-start | bytes 196616 | tf_op jit(solution)/shard_map/ppermute | solution.py:50
  18.8 41.4 %collective-permute-start.1 = (bf16[4,64,128]{2,1,0:T(8,128)(2,1)S(1)}, bf16[4,64,128]{2,1,0:T(8,128)(2,1)S(1)}, u32[]{:S(2)}, u32[]{:S(2)}) collective-permute-start(bf16[4,64,128]{2,1,0:T(8,128)(2,1)S(1)} %get-tuple-element.10), channel_id=1, source_target_pairs={{1,0},{2,1},{3,2},{4,3},{5,4},{6,5},{7,6},{8,7},{9,8},{10,9},{11,1... | collective-permute-start | bytes 196616 | tf_op jit(solution)/shard_map/ppermute | solution.py:51
  20.1 40.1 %collective-permute-start.19 = (bf16[4,64,128]{2,1,0:T(8,128)(2,1)S(1)}, bf16[4,64,128]{2,1,0:T(8,128)(2,1)S(1)}, u32[]{:S(2)}, u32[]{:S(2)}) collective-permute-start(bf16[4,64,128]{2,1,0:T(8,128)(2,1)S(1)} %get-tuple-element.5), channel_id=1, source_target_pairs={{0,1},{1,2},{2,3},{3,4},{4,5},{5,6},{6,7},{7,8},{8,9},{9,10},{10,1... | collective-permute-start | bytes 196616 | tf_op jit(solution)/shard_map/ppermute | solution.py:50
  53.5 6.6 %collective-permute-start.20 = (bf16[4,64,128]{2,1,0:T(8,128)(2,1)S(1)}, bf16[4,64,128]{2,1,0:T(8,128)(2,1)S(1)}, u32[]{:S(2)}, u32[]{:S(2)}) collective-permute-start(bf16[4,64,128]{2,1,0:T(8,128)(2,1)S(1)} %get-tuple-element.6), channel_id=1, source_target_pairs={{1,0},{2,1},{3,2},{4,3},{5,4},{6,5},{7,6},{8,7},{9,8},{10,9},{11,1... | collective-permute-start | bytes 196616 | tf_op jit(solution)/shard_map/ppermute | solution.py:51
  55.7 131.0 %collective-permute-start.6 = (bf16[216,128]{1,0:T(8,128)(2,1)}, bf16[216,128]{1,0:T(8,128)(2,1)S(1)}, u32[]{:S(2)}, u32[]{:S(2)}) collective-permute-start(bf16[216,128]{1,0:T(8,128)(2,1)} %collective-permute-done.4), channel_id=1, source_target_pairs={{0,1},{1,2},{2,3},{3,4},{4,5},{5,6},{6,7},{7,8},{8,9},{9,10},{10,1... | collective-permute-start | bytes 165896 | tf_op jit(solution)/shard_map/ppermute | solution.py:23
  56.8 131.0 %collective-permute-start.7 = (bf16[216,128]{1,0:T(8,128)(2,1)S(1)}, bf16[216,128]{1,0:T(8,128)(2,1)S(1)}, u32[]{:S(2)}, u32[]{:S(2)}) collective-permute-start(bf16[216,128]{1,0:T(8,128)(2,1)S(1)} %collective-permute-done.5), channel_id=1, source_target_pairs={{0,15},{1,0},{2,1},{3,2},{4,3},{5,4},{6,5},{7,6},{8,7},{9,8},{10,9... | collective-permute-start | bytes 165896 | tf_op jit(solution)/shard_map/ppermute | solution.py:32
  173.6 17.5 %collective-permute-start.2 = (bf16[4,64,128]{2,1,0:T(8,128)(2,1)S(1)}, bf16[4,64,128]{2,1,0:T(8,128)(2,1)S(1)}, u32[]{:S(2)}, u32[]{:S(2)}) collective-permute-start(bf16[4,64,128]{2,1,0:T(8,128)(2,1)S(1)} %get-tuple-element.7), channel_id=1, source_target_pairs={{0,1},{1,2},{2,3},{3,4},{4,5},{5,6},{6,7},{7,8},{8,9},{9,10},{10,1... | collective-permute-start | bytes 196616 | tf_op jit(solution)/shard_map/ppermute | solution.py:50
  174.9 16.2 %collective-permute-start.3 = (bf16[4,64,128]{2,1,0:T(8,128)(2,1)S(1)}, bf16[4,64,128]{2,1,0:T(8,128)(2,1)S(1)}, u32[]{:S(2)}, u32[]{:S(2)}) collective-permute-start(bf16[4,64,128]{2,1,0:T(8,128)(2,1)S(1)} %get-tuple-element.8), channel_id=1, source_target_pairs={{1,0},{2,1},{3,2},{4,3},{5,4},{6,5},{7,6},{8,7},{9,8},{10,9},{11,1... | collective-permute-start | bytes 196616 | tf_op jit(solution)/shard_map/ppermute | solution.py:51
  186.6 76.7 %collective-permute-start.8 = (bf16[216,128]{1,0:T(8,128)(2,1)S(1)}, bf16[216,128]{1,0:T(8,128)(2,1)S(1)}, u32[]{:S(2)}, u32[]{:S(2)}) collective-permute-start(bf16[216,128]{1,0:T(8,128)(2,1)S(1)} %collective-permute-done.6), channel_id=1, source_target_pairs={{0,1},{1,2},{2,3},{3,4},{4,5},{5,6},{6,7},{7,8},{8,9},{9,10},{10,1... | collective-permute-start | bytes 165896 | tf_op jit(solution)/shard_map/ppermute | solution.py:23
  187.9 75.5 %collective-permute-start.9 = (bf16[216,128]{1,0:T(8,128)(2,1)S(1)}, bf16[216,128]{1,0:T(8,128)(2,1)S(1)}, u32[]{:S(2)}, u32[]{:S(2)}) collective-permute-start(bf16[216,128]{1,0:T(8,128)(2,1)S(1)} %collective-permute-done.7), channel_id=1, source_target_pairs={{0,15},{1,0},{2,1},{3,2},{4,3},{5,4},{6,5},{7,6},{8,7},{9,8},{10,9... | collective-permute-start | bytes 165896 | tf_op jit(solution)/shard_map/ppermute | solution.py:32
  263.2 122.1 %reduce-scatter.7.cloned.1.call-start = ((), (), s32[]{:S(2)}) async-start(), calls=%async_computation.2 | async-start | bytes 1880064
  263.3 6.3 %collective-permute-start.10 = (bf16[216,128]{1,0:T(8,128)(2,1)S(1)}, bf16[216,128]{1,0:T(8,128)(2,1)S(1)}, u32[]{:S(2)}, u32[]{:S(2)}) collective-permute-start(bf16[216,128]{1,0:T(8,128)(2,1)S(1)} %collective-permute-done.8), channel_id=1, source_target_pairs={{0,1},{1,2},{2,3},{3,4},{4,5},{5,6},{6,7},{7,8},{8,9},{9,10},{10,1... | collective-permute-start | bytes 165896 | tf_op jit(solution)/shard_map/ppermute | solution.py:23
  263.4 6.3 %collective-permute-start.11 = (bf16[216,128]{1,0:T(8,128)(2,1)S(1)}, bf16[216,128]{1,0:T(8,128)(2,1)S(1)}, u32[]{:S(2)}, u32[]{:S(2)}) collective-permute-start(bf16[216,128]{1,0:T(8,128)(2,1)S(1)} %collective-permute-done.9), channel_id=1, source_target_pairs={{0,15},{1,0},{2,1},{3,2},{4,3},{5,4},{6,5},{7,6},{8,7},{9,8},{10,9... | collective-permute-start | bytes 165896 | tf_op jit(solution)/shard_map/ppermute | solution.py:32
  269.6 6.3 %collective-permute-start.12 = (bf16[216,128]{1,0:T(8,128)(2,1)S(1)}, bf16[216,128]{1,0:T(8,128)(2,1)S(1)}, u32[]{:S(2)}, u32[]{:S(2)}) collective-permute-start(bf16[216,128]{1,0:T(8,128)(2,1)S(1)} %collective-permute-done.10), channel_id=1, source_target_pairs={{0,1},{1,2},{2,3},{3,4},{4,5},{5,6},{6,7},{7,8},{8,9},{9,10},{10,1... | collective-permute-start | bytes 165896 | tf_op jit(solution)/shard_map/ppermute | solution.py:23
  269.6 6.3 %collective-permute-start.13 = (bf16[216,128]{1,0:T(8,128)(2,1)S(1)}, bf16[216,128]{1,0:T(8,128)(2,1)S(1)}, u32[]{:S(2)}, u32[]{:S(2)}) collective-permute-start(bf16[216,128]{1,0:T(8,128)(2,1)S(1)} %collective-permute-done.11), channel_id=1, source_target_pairs={{0,15},{1,0},{2,1},{3,2},{4,3},{5,4},{6,5},{7,6},{8,7},{9,8},{10,9... | collective-permute-start | bytes 165896 | tf_op jit(solution)/shard_map/ppermute | solution.py:32
  275.9 6.3 %collective-permute-start.14 = (bf16[216,128]{1,0:T(8,128)(2,1)S(1)}, bf16[216,128]{1,0:T(8,128)(2,1)S(1)}, u32[]{:S(2)}, u32[]{:S(2)}) collective-permute-start(bf16[216,128]{1,0:T(8,128)(2,1)S(1)} %collective-permute-done.12), channel_id=1, source_target_pairs={{0,1},{1,2},{2,3},{3,4},{4,5},{5,6},{6,7},{7,8},{8,9},{9,10},{10,1... | collective-permute-start | bytes 165896 | tf_op jit(solution)/shard_map/ppermute | solution.py:23
  275.9 6.3 %collective-permute-start.15 = (bf16[216,128]{1,0:T(8,128)(2,1)S(1)}, bf16[216,128]{1,0:T(8,128)(2,1)S(1)}, u32[]{:S(2)}, u32[]{:S(2)}) collective-permute-start(bf16[216,128]{1,0:T(8,128)(2,1)S(1)} %collective-permute-done.13), channel_id=1, source_target_pairs={{0,15},{1,0},{2,1},{3,2},{4,3},{5,4},{6,5},{7,6},{8,7},{9,8},{10,9... | collective-permute-start | bytes 165896 | tf_op jit(solution)/shard_map/ppermute | solution.py:32
  282.2 6.3 %collective-permute-start.16 = (bf16[216,128]{1,0:T(8,128)(2,1)S(1)}, bf16[216,128]{1,0:T(8,128)(2,1)S(1)}, u32[]{:S(2)}, u32[]{:S(2)}) collective-permute-start(bf16[216,128]{1,0:T(8,128)(2,1)S(1)} %collective-permute-done.14), channel_id=1, source_target_pairs={{0,1},{1,2},{2,3},{3,4},{4,5},{5,6},{6,7},{7,8},{8,9},{9,10},{10,1... | collective-permute-start | bytes 165896 | tf_op jit(solution)/shard_map/ppermute | solution.py:23
  282.2 6.3 %collective-permute-start.17 = (bf16[216,128]{1,0:T(8,128)(2,1)S(1)}, bf16[216,128]{1,0:T(8,128)(2,1)S(1)}, u32[]{:S(2)}, u32[]{:S(2)}) collective-permute-start(bf16[216,128]{1,0:T(8,128)(2,1)S(1)} %collective-permute-done.15), channel_id=1, source_target_pairs={{0,15},{1,0},{2,1},{3,2},{4,3},{5,4},{6,5},{7,6},{8,7},{9,8},{10,9... | collective-permute-start | bytes 165896 | tf_op jit(solution)/shard_map/ppermute | solution.py:32
  288.5 7.1 %collective-permute-start.18 = (bf16[216,128]{1,0:T(8,128)(2,1)S(1)}, bf16[216,128]{1,0:T(8,128)(2,1)S(1)}, u32[]{:S(2)}, u32[]{:S(2)}) collective-permute-start(bf16[216,128]{1,0:T(8,128)(2,1)S(1)} %collective-permute-done.16), channel_id=1, source_target_pairs={{0,1},{1,2},{2,3},{3,4},{4,5},{5,6},{6,7},{7,8},{8,9},{9,10},{10,1... | collective-permute-start | bytes 165896 | tf_op jit(solution)/shard_map/ppermute | solution.py:23
  (5 other events, 162.6 us)
Sparse Core Ops, SparseCore 0:
  263.3 58.4 reduce-scatter.8
  326.1 59.1 reduce-scatter.6
